TPU v7x, 32 devices: a whole 2x2x4 slice. The times are simulated.
32 devices in a mesh: mode: 8 (over z, core), dom: 4 (over y, x).
Axes of the slice: x: 2, y: 2, z: 4, core: 2. Of those that a mesh axis runs over, the one named last changes fastest.
Arguments:
- velocity: float32 [3, 128, 2, 8192], P(None, 'mode', None, 'dom'), may hold values from -0.375 to 0.375
- vorticity: float32 [3, 128, 2, 8192], P(None, 'mode', None, 'dom'), may hold values from -0.375 to 0.375
- blocks: float32 [9, 64, 64], replicated, may hold values from -0.042 to 0.042
- nbr_ref: int32 [9, 128], P(None, 'dom'), may hold values from 0 to 47
- send_list: int32 [2, 32], P(None, 'dom'), may hold values from 0 to 31
Outputs:
- velocity_new: float32 [3, 128, 2, 8192], P(None, 'mode', None, 'dom')
Inputs may be any that keep to these rules, and one draw needn't show every extreme that they name: nbr_ref indexes the extended list of the element's own partition; partitions form a cycle. send_list holds local element numbers of the partition that holds the entry.
All inputs are finite; a program needn't handle non-finite values.
Results may differ from a plain program's by a relative error of at most 0.0001.
Values sent between devices are 32-bit elements; how exact they have to be, the bound alone decides.
A program may use at most 64 MiB of HBM per device.

v0:
```python
import functools

import jax
import jax.numpy as jnp
import numpy as np
from jax import lax
from jax.experimental import pallas as pl
from jax.experimental.pallas import tpu as pltpu
from jax.sharding import PartitionSpec as P

CHEB = 4
F32 = jnp.float32
BF16 = jnp.bfloat16


def split(value):
    high = value.astype(BF16)
    return high, (value - high.astype(F32)).astype(BF16)


def dot(left, right):
    return jnp.dot(left, right, preferred_element_type=F32)


def dot3(left_high, left_low, right):
    high, low = split(right)
    return dot(left_high, high) + dot(left_high, low) + dot(left_low, high)


def spanwise_tables(count):
    phase = np.arange(2 * count)[:, None] * np.arange(count)[None, :] % (2 * count)
    angle = 2.0 * np.pi / (2 * count) * phase
    weights = np.where(np.arange(count) == 0, 1.0, 2.0)[None, :, None]
    waves = np.stack([np.cos(angle), -np.sin(angle)], axis=2)
    forward = (weights * waves).reshape(2 * count, 2 * count).astype(np.float32)
    back = (waves / (2 * count)).reshape(2 * count, 2 * count).T.astype(np.float32)
    tables = []
    for table in (forward, back):
        high = table.astype(jnp.bfloat16)
        tables += [high, (table - high.astype(np.float32)).astype(jnp.bfloat16)]
    return tables


def lines_kernel(chunk, lines, inv_high, inv_low, back_high, back_low, diag, out):
    count = diag.shape[0]
    columns = lines.shape[-1]
    planes = []
    for field in range(2):
        for part in range(3):
            value = lines[:, field, part].reshape(count, columns)
            planes.append(dot3(inv_high[...], inv_low[...], value))
    for part in range(3):
        one, two = (part + 1) % 3, (part + 2) % 3
        cross = planes[one] * planes[3 + two] - planes[two] * planes[3 + one]
        forcing = dot3(back_high[...], back_low[...], cross)
        rhs = (lines[:, 0, part].reshape(count, columns) + forcing) * diag[...]
        if chunk % 8 == 0:
            out[:, part * chunk : (part + 1) * chunk, :] = rhs.reshape(count // chunk, chunk, columns)
        else:
            out[part] = rhs


def cheb_kernel(group, sides, refs, rhs, weights, scale, out, fields, resid, solution, rows_in, wide):
    sources, rows, columns = rhs.shape
    per_source = columns // 64
    elems = sources * per_source
    slots = rows_in.shape[1] // 64
    lane = lax.broadcasted_iota(jnp.int32, (1, 1, 128), 2)
    lower = lane < 64
    first, second = fields.at[0], fields.at[1]
    wide[:, :128], wide[:, 128:] = split(weights[...])
    for half in range(columns // 128):
        both = rhs[:, :, half * 128 : (half + 1) * 128]
        turned = pltpu.roll(both, 64, axis=2)
        first[:, 2 * half] = jnp.where(lower, both, turned)
        first[:, 2 * half + 1] = jnp.where(lower, turned, both)

    rho = 0.5
    for step in range(CHEB):
        now, later = (first, second) if step % 2 == 0 else (second, first)
        rho_next = 1.0 / (4.0 - rho)
        last = step == CHEB - 1

        def body(index, carry, step=step, now=now, later=later, rho=rho, rho_next=rho_next, last=last):
            low_lane = lower[0]
            for j in range(group):
                elem = index * group + j
                for pair in range(slots // 2):
                    a = refs[2 * pair, elem]
                    b = refs[2 * pair + 1, elem]
                    left = now[a // per_source, a % per_source]
                    right = now[b // per_source, b % per_source]
                    rows_in[j * rows : (j + 1) * rows, pair * 128 : (pair + 1) * 128] = jnp.where(
                        low_lane, left, right
                    )
            high, low = split(rows_in[...])
            total = dot(high, wide[...])
            total = total[:, :128] + total[:, 128:] + dot(low, wide[:, :128])
            total = total.reshape(group // per_source, per_source, rows, 128)
            here = pl.ds(index * (group // per_source), group // per_source)
            direction = now[here]
            old = direction if step == 0 else resid[here]
            new = old - (direction + scale[...] * total)
            ahead = rho_next * rho * direction + 4.0 * rho_next * new
            so_far = direction if step == 0 else solution[here] + direction
            if last:
                solution[here] = so_far + ahead
            else:
                resid[here] = new
                solution[here] = so_far
                later[here] = ahead
            return carry

        lax.fori_loop(0, elems // group, body, 0)
        rho = rho_next

    for behind in range(sources // sides):
        for half in range(columns // 128):
            at = behind * columns + half * 128
            here = pl.ds(behind * sides, sides)
            out[:, :, at : at + 128] = jnp.where(
                lower, solution[here, 2 * half], solution[here, 2 * half + 1]
            )


def shards(velocity, vorticity, blocks, nbr_ref, send_list):
    slot_count, points, _ = blocks.shape
    modes_dev, merged = velocity.shape[1], velocity.shape[3]
    mode_size, dom_size = lax.axis_size("mode"), lax.axis_size("dom")
    devices = mode_size * dom_size
    modes_all = modes_dev * mode_size
    count = 2 * modes_all
    columns = merged // mode_size
    elem_local = merged // points
    per_source = columns // points
    chunk = count // devices
    rows = 3 * chunk
    rows_up = -(-rows // 8) * 8

    tables = jnp.concatenate([nbr_ref.reshape(-1), send_list.reshape(-1)])
    tables = lax.all_gather(tables, "dom")
    refs = tables[:, : slot_count * elem_local].reshape(dom_size, slot_count, elem_local)
    lists = tables[:, slot_count * elem_local :].reshape(dom_size, 2, -1)
    doms = jnp.arange(dom_size, dtype=jnp.int32)[:, None]
    own = jnp.broadcast_to(jnp.arange(elem_local, dtype=jnp.int32)[None], (dom_size, elem_local))

    def place(dom, elem):
        return ((elem // per_source) * dom_size + dom) * per_source + elem % per_source

    extended = jnp.concatenate(
        [
            place(doms, own),
            jnp.roll(place(doms, lists[:, 0]), 1, axis=0),
            jnp.roll(place(doms, lists[:, 1]), -1, axis=0),
        ],
        axis=1,
    )
    entries = jnp.arange(extended.shape[1], dtype=jnp.int32)
    chosen = jnp.sum(
        jnp.where(refs[..., None] == entries, extended[:, None, None, :], 0), axis=-1
    )
    chosen = jnp.pad(chosen, ((0, 0), (0, slot_count % 2), (0, 0)))
    slots = chosen.shape[1]
    chosen = chosen.reshape(dom_size, slots, mode_size, per_source).transpose(1, 2, 0, 3)
    chosen = chosen.reshape(slots, devices * per_source)

    weights = jnp.swapaxes(blocks, 1, 2).reshape(slot_count * points, points)
    weights = jnp.pad(weights, ((0, (slots - slot_count) * points), (0, 0)))
    weights = jnp.concatenate([weights] * 2, axis=1)

    wavenum = np.arange(modes_all, dtype=np.float32) / np.float32(modes_all)
    inv_diag = np.repeat(np.float32(1.0) / (np.float32(1.0) + np.float32(4.0) * wavenum * wavenum), 2)

    both = jnp.stack([velocity, vorticity]).reshape(6 * modes_dev * 2, mode_size, columns)
    both = jnp.swapaxes(both, 0, 1)
    both = lax.all_to_all(both, "mode", split_axis=0, concat_axis=0, tiled=True)
    lines = both.reshape(mode_size, 2, 3, 2 * modes_dev, columns)

    aligned = chunk % 8 == 0
    rhs = pl.pallas_call(
        functools.partial(lines_kernel, chunk),
        out_shape=jax.ShapeDtypeStruct(
            (devices, rows, columns) if aligned else (3, count, columns), F32
        ),
        compiler_params=pltpu.CompilerParams(vmem_limit_bytes=40 * 2**20),
    )(lines, *(jnp.asarray(t) for t in spanwise_tables(modes_all)), jnp.asarray(inv_diag[:, None]))
    if not aligned:
        rhs = jnp.swapaxes(rhs.reshape(3, devices, chunk, columns), 0, 1).reshape(devices, rows, columns)
    rhs = lax.all_to_all(rhs, ("mode", "dom"), split_axis=0, concat_axis=0, tiled=True)
    if rows_up != rows:
        rhs = jnp.pad(rhs, ((0, 0), (0, rows_up - rows), (0, 0)))

    me = lax.axis_index("mode") * dom_size + lax.axis_index("dom")
    mode_ids = (me * chunk + jnp.arange(chunk, dtype=jnp.int32)) // 2
    wave = mode_ids.astype(F32) / modes_all
    scale = jnp.tile(1.0 / (1.0 + 4.0 * wave * wave), 3)
    scale = jnp.pad(scale, (0, rows_up - rows))
    scale = jnp.broadcast_to(scale[:, None], (rows_up, 128))

    group = 2 * per_source
    held = (devices, per_source, rows_up, 128)
    vmem = pl.BlockSpec(memory_space=pltpu.VMEM)
    out = pl.pallas_call(
        functools.partial(cheb_kernel, group, dom_size),
        out_shape=jax.ShapeDtypeStruct((dom_size, rows_up, merged), F32),
        in_specs=[pl.BlockSpec(memory_space=pltpu.SMEM)] + [vmem] * 3,
        out_specs=vmem,
        scratch_shapes=[
            pltpu.VMEM((2, *held), F32),
            pltpu.VMEM(held, F32),
            pltpu.VMEM(held, F32),
            pltpu.VMEM((group * rows_up, slots * points), F32),
            pltpu.VMEM((slots * points, 256), BF16),
        ],
        compiler_params=pltpu.CompilerParams(vmem_limit_bytes=48 * 2**20),
    )(chosen, rhs, weights, scale)
    out = lax.all_to_all(out[:, :rows], "dom", split_axis=0, concat_axis=0, tiled=True)
    out = jnp.swapaxes(out.reshape(dom_size, 3, chunk, merged), 0, 1)
    return out.reshape(3, modes_dev, 2, merged)


def solution(mesh):
    placed = (
        P(None, "mode", None, "dom"),
        P(None, "mode", None, "dom"),
        P(),
        P(None, "dom"),
        P(None, "dom"),
    )
    return jax.shard_map(
        shards, mesh=mesh, in_specs=placed, out_specs=P(None, "mode", None, "dom"), check_vma=False
    )
```

profile of v0, /device:TPU:0, one launch (start us, length us, event | category | flops | bytes accessed | tf_op | source)
XLA Modules:
  0.0 138.9 jit_solution(16133260374378327534)
XLA Ops:
  0.0 2.2 %pad_maximum_fusion = f32[2,3,16,2,2048]{4,3,2,1,0:T(2,128)S(1)} fusion(f32[1,3,16,2,2048]{4,3,2,1,0:T(2,128)} %bitcast.26, f32[1,3,16,2,2048]{4,3,2,1,0:T(2,128)} %bitcast.27), kind=kLoop, calls=%fused_computation | loop fusion | flops 393216 | bytes 3145728 | tf_op jit(solution)/shard_map/stack | solution.py:174
  2.2 1.3 reshape.64
  3.4 1.6 %copy.27 = f32[192,8,256]{2,0,1:T(8,128)} copy(f32[192,8,256]{2,1,0:T(8,128)S(1)} %reshape.64) | data formatting | bytes 3145728 | tf_op jit(solution)/shard_map/reshape | solution.py:174
  5.1 0.0 copy-start.7
  5.1 0.0 copy-start.6
  5.1 0.0 copy-start.8
  5.1 0.0 copy-start
  5.1 0.0 copy-start.1
  5.1 0.0 copy-start.2
  5.1 0.0 copy-start.3
  5.1 0.0 copy-start.4
  5.1 6.5 %all-to-all-start = ((f32[8,192,256]{2,1,0:T(8,128)}), f32[8,192,256]{2,1,0:T(8,128)S(1)}, u32[]{:S(2)}, u32[]{:S(2)}) async-start(f32[8,192,256]{2,1,0:T(8,128)} %bitcast.23), calls=%async_computation | async-start | bytes 3145728 | tf_op jit(solution)/shard_map/all_to_all | solution.py:176
  11.6 0.0 copy-done.7
  11.6 0.1 reshape.60
  11.7 0.0 copy-done.6
  11.7 0.1 reshape.59
  11.8 0.0 copy-done.8
  11.8 0.6 dynamic-slice
  13.0 0.2 add_dynamic-update-slice_fusion
  13.2 7.5 %all-reduce.2 = s32[1216]{0:T(1024)S(1)} all-reduce(s32[1216]{0:T(1024)S(1)} %add_dynamic-update-slice_fusion), channel_id=2, replica_groups=mesh['mode'=8,'dom'=4] {'dom'}, use_global_device_ids=true, to_apply=%add.2 | all-reduce | flops 1216 | bytes 9728
  20.7 0.1 reshape.69
  20.8 0.1 slice.37
  20.9 0.1 reshape.61
  20.9 28.5 %all-to-all-done = f32[8,192,256]{2,1,0:T(8,128)S(1)} async-done(((f32[8,192,256]{2,1,0:T(8,128)}), f32[8,192,256]{2,1,0:T(8,128)S(1)}, u32[]{:S(2)}, u32[]{:S(2)}) %all-to-all-start) | async-done | bytes 1572896 | tf_op jit(solution)/shard_map/all_to_all | solution.py:176
  49.4 0.0 copy-done
  49.4 0.0 copy-done.1
  49.5 0.0 copy-done.2
  49.5 0.0 copy-done.3
  49.5 0.0 copy-done.4
  49.5 2.3 %shard_map.100 = f32[32,24,256]{2,1,0:T(8,128)} custom-call(f32[8,2,3,32,256]{4,3,2,1,0:T(8,128)S(1)} %bitcast.22, bf16[256,256]{1,0:T(8,128)(2,1)S(1)} %copy-done, bf16[256,256]{1,0:T(8,128)(2,1)S(1)} %copy-done.1, bf16[256,256]{1,0:T(8,128)(2,1)S(1)} %copy-done.2, bf16[256,256]{1,0:T(8,128)(2,1)S(1)} %copy-done.3, f32[256,1]{1,0:T(8,128)S(1)} %copy-done.4), custom_call_target="tpu_custom_call" | custom-call | tf_op jit(solution)/shard_map/pallas_call | solution.py:180
  51.8 0.0 copy-start.5
  51.8 3.5 %all-to-all-start.1 = ((f32[32,24,256]{2,1,0:T(8,128)}), f32[32,24,256]{2,1,0:T(8,128)S(1)}, u32[]{:S(2)}, u32[]{:S(2)}) async-start(f32[32,24,256]{2,1,0:T(8,128)} %shard_map.100), calls=%async_computation.1 | async-start | bytes 1572864 | tf_op jit(solution)/shard_map/all_to_all | solution.py:189
  55.4 0.1 eq.20
  55.5 0.1 add_add_fusion
  55.6 0.9 select_reduce_fusion
  56.5 0.1 copy.25
  56.6 0.1 copy.23.refs
  56.7 0.0 copy-done.5
  56.7 0.2 copy.22
  56.9 0.1 broadcast_in_dim.47
  57.0 0.2 pad_maximum_fusion.1.weights
  57.2 19.6 %all-to-all-done.1.rhs = f32[32,24,256]{2,1,0:T(8,128)S(1)} async-done(((f32[32,24,256]{2,1,0:T(8,128)}), f32[32,24,256]{2,1,0:T(8,128)S(1)}, u32[]{:S(2)}, u32[]{:S(2)}) %all-to-all-start.1) | async-done | bytes 786464 | tf_op jit(solution)/shard_map/all_to_all | solution.py:189
  76.7 0.1 broadcast_in_dim.48.scale
  76.8 46.9 %shard_map.101 = f32[4,24,2048]{2,1,0:T(8,128)S(1)} custom-call(s32[10,128]{1,0:T(8,128)S(1)} %copy.23.refs, f32[32,24,256]{2,1,0:T(8,128)S(1)} %all-to-all-done.1.rhs, f32[640,128]{1,0:T(8,128)S(1)} %pad_maximum_fusion.1.weights, f32[24,128]{1,0:T(8,128)S(1)} %broadcast_in_dim.48.scale), custom_call_target="tpu_custom_call" | custom-call | tf_op jit(solution)/shard_map/pallas_call | solution.py:203
  123.7 13.9 %all_to_all.15 = f32[4,24,2048]{2,1,0:T(8,128)S(1)} all-to-all(f32[4,24,2048]{2,1,0:T(8,128)S(1)} %shard_map.101), channel_id=1, replica_groups=mesh['mode'=8,'dom'=4] {'dom'}, dimensions={0} | all-to-all | bytes 1572864 | tf_op jit(solution)/shard_map/all_to_all | solution.py:217
  137.5 0.1 copy.24
  137.6 1.3 reshape.68
  (16 shorter events, 0.1 us)
Async XLA Ops:
  5.1 6.5 %copy-start.7 = (s32[2,8]{1,0:T(2,128)S(1)}, s32[2,8]{1,0:T(2,128)}, u32[]{:S(2)}) copy-start(s32[2,8]{1,0:T(2,128)} %param.14) | copy-start | bytes 196
  5.1 6.6 %copy-start.6 = (s32[9,32]{1,0:T(8,128)S(1)}, s32[9,32]{1,0:T(8,128)}, u32[]{:S(2)}) copy-start(s32[9,32]{1,0:T(8,128)} %param.13) | copy-start | bytes 3460
  5.1 6.7 %copy-start.8 = (u32[32]{0:T(128)S(1)}, u32[32]{0:T(128)}, u32[]{:S(2)}) copy-start(u32[32]{0:T(128)} %constant.118) | copy-start | bytes 388
  5.1 44.4 %copy-start = (bf16[256,256]{1,0:T(8,128)(2,1)S(1)}, bf16[256,256]{1,0:T(8,128)(2,1)}, u32[]{:S(2)}) copy-start(bf16[256,256]{1,0:T(8,128)(2,1)} %constant.107.clone.inv_high) | copy-start | bytes 393220
  5.1 44.4 %copy-start.1 = (bf16[256,256]{1,0:T(8,128)(2,1)S(1)}, bf16[256,256]{1,0:T(8,128)(2,1)}, u32[]{:S(2)}) copy-start(bf16[256,256]{1,0:T(8,128)(2,1)} %constant.108.clone.inv_low) | copy-start | bytes 393220
  5.1 44.3 %copy-start.2 = (bf16[256,256]{1,0:T(8,128)(2,1)S(1)}, bf16[256,256]{1,0:T(8,128)(2,1)}, u32[]{:S(2)}) copy-start(bf16[256,256]{1,0:T(8,128)(2,1)} %constant.109.clone.back_high) | copy-start | bytes 393220
  5.1 44.3 %copy-start.3 = (bf16[256,256]{1,0:T(8,128)(2,1)S(1)}, bf16[256,256]{1,0:T(8,128)(2,1)}, u32[]{:S(2)}) copy-start(bf16[256,256]{1,0:T(8,128)(2,1)} %constant.110.clone.back_low) | copy-start | bytes 393220
  5.1 44.3 %copy-start.4 = (f32[256,1]{1,0:T(8,128)S(1)}, f32[256,1]{1,0:T(8,128)}, u32[]{:S(2)}) copy-start(f32[256,1]{1,0:T(8,128)} %constant.111.clone.diag) | copy-start | bytes 3076
  5.1 44.3 %all-to-all-start = ((f32[8,192,256]{2,1,0:T(8,128)}), f32[8,192,256]{2,1,0:T(8,128)S(1)}, u32[]{:S(2)}, u32[]{:S(2)}) async-start(f32[8,192,256]{2,1,0:T(8,128)} %bitcast.23), calls=%async_computation | async-start | bytes 3145728 | tf_op jit(solution)/shard_map/all_to_all | solution.py:176
  51.8 4.9 %copy-start.5 = (f32[9,64,64]{2,1,0:T(8,128)S(1)}, f32[9,64,64]{2,1,0:T(8,128)}, u32[]{:S(2)}) copy-start(f32[9,64,64]{2,1,0:T(8,128)} %param.12) | copy-start | bytes 442372
  51.8 24.9 %all-to-all-start.1 = ((f32[32,24,256]{2,1,0:T(8,128)}), f32[32,24,256]{2,1,0:T(8,128)S(1)}, u32[]{:S(2)}, u32[]{:S(2)}) async-start(f32[32,24,256]{2,1,0:T(8,128)} %shard_map.100), calls=%async_computation.1 | async-start | bytes 1572864 | tf_op jit(solution)/shard_map/all_to_all | solution.py:189
where the time goes:
time: 139 us
  Pallas kernels  49.2 us (35%)
  waiting for transfers between devices  48.1 us (35%)
  blocking collectives  21.4 us (15%)
  starting transfers between devices  9.98 us (7%)
  local copies, waits for them, and re-layouts  5.94 us (4%)
  other arithmetic  3.53 us (3%)
    pallas_call x1, Pallas kernels, shards(): pl.pallas_call(functools.partial(cheb_kernel, group, dom_size), out_shape...  46.9 us
    all_to_all x1, waiting for transfers between devices, shards(): both = lax.all_to_all(both, 'mode', split_axis=0, concat_axis=0, tiled=True)  28.5 us
    all_to_all x1, waiting for transfers between devices, shards(): lax.all_to_all(rhs, ('mode', 'dom'), split_axis=0, concat_axis=0, tiled=T...  19.6 us
    all_to_all x1, blocking collectives, shards(): lax.all_to_all(out[:, :rows], 'dom', split_axis=0, concat_axis=0, tiled=T...  13.9 us
    unnamed x1, blocking collectives  7.48 us
    all_to_all x1, starting transfers between devices, shards(): both = lax.all_to_all(both, 'mode', split_axis=0, concat_axis=0, tiled=True)  6.47 us
    all_to_all x1, starting transfers between devices, shards(): lax.all_to_all(rhs, ('mode', 'dom'), split_axis=0, concat_axis=0, tiled=T...  3.51 us
    reshape x2, local copies, waits for them, and re-layouts, shards(): jnp.stack([velocity, vorticity])  2.89 us
  transfers between devices with their start and end apart: 2, of which 2 were waited for; matrix products, arithmetic and copies ran while one was open for 2% of the time, Pallas kernels for 0%

commit v1 on v0

--- a/solution.py
+++ b/solution.py
@@ -72,8 +72,9 @@
     for half in range(columns // 128):
         both = rhs[:, :, half * 128 : (half + 1) * 128]
         turned = pltpu.roll(both, 64, axis=2)
-        first[:, 2 * half] = jnp.where(lower, both, turned)
-        first[:, 2 * half + 1] = jnp.where(lower, turned, both)
+        at = 2 * half * sources
+        first[at : at + sources] = jnp.where(lower, both, turned)
+        first[at + sources : at + 2 * sources] = jnp.where(lower, turned, both)
 
     rho = 0.5
     for step in range(CHEB):
@@ -88,16 +89,16 @@
                 for pair in range(slots // 2):
                     a = refs[2 * pair, elem]
                     b = refs[2 * pair + 1, elem]
-                    left = now[a // per_source, a % per_source]
-                    right = now[b // per_source, b % per_source]
+                    left = now[a]
+                    right = now[b]
                     rows_in[j * rows : (j + 1) * rows, pair * 128 : (pair + 1) * 128] = jnp.where(
                         low_lane, left, right
                     )
             high, low = split(rows_in[...])
             total = dot(high, wide[...])
             total = total[:, :128] + total[:, 128:] + dot(low, wide[:, :128])
-            total = total.reshape(group // per_source, per_source, rows, 128)
-            here = pl.ds(index * (group // per_source), group // per_source)
+            total = total.reshape(group, rows, 128)
+            here = pl.ds(index * group, group)
             direction = now[here]
             old = direction if step == 0 else resid[here]
             new = old - (direction + scale[...] * total)
@@ -117,10 +118,9 @@
     for behind in range(sources // sides):
         for half in range(columns // 128):
             at = behind * columns + half * 128
-            here = pl.ds(behind * sides, sides)
-            out[:, :, at : at + 128] = jnp.where(
-                lower, solution[here, 2 * half], solution[here, 2 * half + 1]
-            )
+            even = pl.ds(2 * half * sources + behind * sides, sides)
+            odd = pl.ds((2 * half + 1) * sources + behind * sides, sides)
+            out[:, :, at : at + 128] = jnp.where(lower, solution[even], solution[odd])
 
 
 def shards(velocity, vorticity, blocks, nbr_ref, send_list):
@@ -145,7 +145,7 @@
     own = jnp.broadcast_to(jnp.arange(elem_local, dtype=jnp.int32)[None], (dom_size, elem_local))
 
     def place(dom, elem):
-        return ((elem // per_source) * dom_size + dom) * per_source + elem % per_source
+        return (elem % per_source) * devices + (elem // per_source) * dom_size + dom
 
     extended = jnp.concatenate(
         [
@@ -161,7 +161,7 @@
     )
     chosen = jnp.pad(chosen, ((0, 0), (0, slot_count % 2), (0, 0)))
     slots = chosen.shape[1]
-    chosen = chosen.reshape(dom_size, slots, mode_size, per_source).transpose(1, 2, 0, 3)
+    chosen = chosen.reshape(dom_size, slots, mode_size, per_source).transpose(1, 3, 2, 0)
     chosen = chosen.reshape(slots, devices * per_source)
 
     weights = jnp.swapaxes(blocks, 1, 2).reshape(slot_count * points, points)
@@ -197,8 +197,8 @@
     scale = jnp.pad(scale, (0, rows_up - rows))
     scale = jnp.broadcast_to(scale[:, None], (rows_up, 128))
 
-    group = 2 * per_source
-    held = (devices, per_source, rows_up, 128)
+    group = min(32, devices)
+    held = (devices * per_source, rows_up, 128)
     vmem = pl.BlockSpec(memory_space=pltpu.VMEM)
     out = pl.pallas_call(
         functools.partial(cheb_kernel, group, dom_size),

time: 139 us -> 106 us (0.76)
  Pallas kernels: 49.2 us -> 16.3 us
    pallas_call x1, Pallas kernels: 46.9 us -> 14 us  [shards(): pl.pallas_call(functools.partial(cheb_kernel, group, dom_size), out_shape...]
  transfers between devices with their start and end apart: 2 -> 2, of which waited for: 2 -> 2; matrix products, arithmetic and copies ran while one was open for 2% -> 3% of each run, Pallas kernels for 0% -> 0%
where the time goes in v1:
time: 106 us
  waiting for transfers between devices  48 us (45%)
  blocking collectives  21.4 us (20%)
  Pallas kernels  16.3 us (15%)
  starting transfers between devices  9.98 us (9%)
  local copies, waits for them, and re-layouts  5.98 us (6%)
  other arithmetic  3.53 us (3%)
    all_to_all x1, waiting for transfers between devices, shards(): both = lax.all_to_all(both, 'mode', split_axis=0, concat_axis=0, tiled=True)  28.5 us
    all_to_all x1, waiting for transfers between devices, shards(): lax.all_to_all(rhs, ('mode', 'dom'), split_axis=0, concat_axis=0, tiled=T...  19.5 us
    pallas_call x1, Pallas kernels, shards(): pl.pallas_call(functools.partial(cheb_kernel, group, dom_size), out_shape...  14 us
    all_to_all x1, blocking collectives, shards(): lax.all_to_all(out[:, :rows], 'dom', split_axis=0, concat_axis=0, tiled=T...  13.9 us
    unnamed x1, blocking collectives  7.48 us
    all_to_all x1, starting transfers between devices, shards(): both = lax.all_to_all(both, 'mode', split_axis=0, concat_axis=0, tiled=True)  6.47 us
    all_to_all x1, starting transfers between devices, shards(): lax.all_to_all(rhs, ('mode', 'dom'), split_axis=0, concat_axis=0, tiled=T...  3.51 us
    reshape x2, local copies, waits for them, and re-layouts, shards(): jnp.stack([velocity, vorticity])  2.89 us
  transfers between devices with their start and end apart: 2, of which 2 were waited for; matrix products, arithmetic and copies ran while one was open for 3% of the time, Pallas kernels for 0%

profile of v1, /device:TPU:0, one launch (start us, length us, event | category | flops | bytes accessed | tf_op | source)
XLA Modules:
  0.0 106.1 jit_solution(8382174107791683272)
XLA Ops:
  0.0 2.2 %pad_maximum_fusion = f32[2,3,16,2,2048]{4,3,2,1,0:T(2,128)S(1)} fusion(f32[1,3,16,2,2048]{4,3,2,1,0:T(2,128)} %bitcast.26, f32[1,3,16,2,2048]{4,3,2,1,0:T(2,128)} %bitcast.27), kind=kLoop, calls=%fused_computation | loop fusion | flops 393216 | bytes 3145728 | tf_op jit(solution)/shard_map/stack | solution.py:174
  2.2 1.3 %reshape.64 = f32[192,8,256]{2,1,0:T(8,128)S(1)} reshape(f32[2,3,16,2,2048]{4,3,2,1,0:T(2,128)S(1)} %pad_maximum_fusion) | data formatting | bytes 3145728 | tf_op jit(solution)/shard_map/reshape | solution.py:174
  3.4 1.6 %copy.27 = f32[192,8,256]{2,0,1:T(8,128)} copy(f32[192,8,256]{2,1,0:T(8,128)S(1)} %reshape.64) | data formatting | bytes 3145728 | tf_op jit(solution)/shard_map/reshape | solution.py:174
  5.1 0.0 copy-start.7
  5.1 0.0 copy-start.6
  5.1 0.0 copy-start.8
  5.1 0.0 copy-start
  5.1 0.0 copy-start.1
  5.1 0.0 copy-start.2
  5.1 0.0 copy-start.3
  5.1 0.0 copy-start.4
  5.1 6.5 %all-to-all-start = ((f32[8,192,256]{2,1,0:T(8,128)}), f32[8,192,256]{2,1,0:T(8,128)S(1)}, u32[]{:S(2)}, u32[]{:S(2)}) async-start(f32[8,192,256]{2,1,0:T(8,128)} %bitcast.23), calls=%async_computation | async-start | bytes 3145728 | tf_op jit(solution)/shard_map/all_to_all | solution.py:176
  11.6 0.0 copy-done.7
  11.6 0.1 reshape.60
  11.7 0.0 copy-done.6
  11.7 0.1 reshape.59
  11.8 0.0 copy-done.8
  11.8 0.6 dynamic-slice
  13.0 0.2 add_dynamic-update-slice_fusion
  13.2 7.5 %all-reduce.2 = s32[1216]{0:T(1024)S(1)} all-reduce(s32[1216]{0:T(1024)S(1)} %add_dynamic-update-slice_fusion), channel_id=2, replica_groups=mesh['mode'=8,'dom'=4] {'dom'}, use_global_device_ids=true, to_apply=%add.2 | all-reduce | flops 1216 | bytes 9728
  20.7 0.1 reshape.69
  20.8 0.1 slice.37
  20.9 0.1 reshape.61
  20.9 28.5 %all-to-all-done = f32[8,192,256]{2,1,0:T(8,128)S(1)} async-done(((f32[8,192,256]{2,1,0:T(8,128)}), f32[8,192,256]{2,1,0:T(8,128)S(1)}, u32[]{:S(2)}, u32[]{:S(2)}) %all-to-all-start) | async-done | bytes 1572896 | tf_op jit(solution)/shard_map/all_to_all | solution.py:176
  49.4 0.0 copy-done
  49.4 0.0 copy-done.1
  49.5 0.0 copy-done.2
  49.5 0.0 copy-done.3
  49.5 0.0 copy-done.4
  49.5 2.3 %shard_map.100 = f32[32,24,256]{2,1,0:T(8,128)} custom-call(f32[8,2,3,32,256]{4,3,2,1,0:T(8,128)S(1)} %bitcast.22, bf16[256,256]{1,0:T(8,128)(2,1)S(1)} %copy-done, bf16[256,256]{1,0:T(8,128)(2,1)S(1)} %copy-done.1, bf16[256,256]{1,0:T(8,128)(2,1)S(1)} %copy-done.2, bf16[256,256]{1,0:T(8,128)(2,1)S(1)} %copy-done.3, f32[256,1]{1,0:T(8,128)S(1)} %copy-done.4), custom_call_target="tpu_custom_call" | custom-call | tf_op jit(solution)/shard_map/pallas_call | solution.py:180
  51.8 0.0 copy-start.5
  51.8 3.5 %all-to-all-start.1 = ((f32[32,24,256]{2,1,0:T(8,128)}), f32[32,24,256]{2,1,0:T(8,128)S(1)}, u32[]{:S(2)}, u32[]{:S(2)}) async-start(f32[32,24,256]{2,1,0:T(8,128)} %shard_map.100), calls=%async_computation.1 | async-start | bytes 1572864 | tf_op jit(solution)/shard_map/all_to_all | solution.py:189
  55.4 0.1 eq.20
  55.5 0.1 add_add_fusion
  55.6 0.9 select_reduce_fusion
  56.5 0.1 copy.25
  56.7 0.1 copy.23.refs
  56.7 0.0 copy-done.5
  56.7 0.2 copy.22
  56.9 0.1 broadcast_in_dim.47
  57.0 0.2 pad_maximum_fusion.1.weights
  57.2 19.5 %all-to-all-done.1.rhs = f32[32,24,256]{2,1,0:T(8,128)S(1)} async-done(((f32[32,24,256]{2,1,0:T(8,128)}), f32[32,24,256]{2,1,0:T(8,128)S(1)}, u32[]{:S(2)}, u32[]{:S(2)}) %all-to-all-start.1) | async-done | bytes 786464 | tf_op jit(solution)/shard_map/all_to_all | solution.py:189
  76.7 0.1 broadcast_in_dim.48.scale
  76.8 14.0 %shard_map.101 = f32[4,24,2048]{2,1,0:T(8,128)S(1)} custom-call(s32[10,128]{1,0:T(8,128)S(1)} %copy.23.refs, f32[32,24,256]{2,1,0:T(8,128)S(1)} %all-to-all-done.1.rhs, f32[640,128]{1,0:T(8,128)S(1)} %pad_maximum_fusion.1.weights, f32[24,128]{1,0:T(8,128)S(1)} %broadcast_in_dim.48.scale), custom_call_target="tpu_custom_call" | custom-call | tf_op jit(solution)/shard_map/pallas_call | solution.py:203
  90.8 13.9 %all_to_all.15 = f32[4,24,2048]{2,1,0:T(8,128)S(1)} all-to-all(f32[4,24,2048]{2,1,0:T(8,128)S(1)} %shard_map.101), channel_id=1, replica_groups=mesh['mode'=8,'dom'=4] {'dom'}, dimensions={0} | all-to-all | bytes 1572864 | tf_op jit(solution)/shard_map/all_to_all | solution.py:217
  104.7 0.1 copy.24
  104.7 1.3 %reshape.68 = f32[3,16,2,2048]{3,2,1,0:T(2,128)} reshape(f32[3,4,8,2048]{3,2,1,0:T(8,128)S(1)} %copy.24) | data formatting | bytes 1572864 | tf_op jit(solution)/shard_map/reshape | solution.py:219
  (16 shorter events, 0.2 us)
Async XLA Ops:
  5.1 6.5 %copy-start.7 = (s32[2,8]{1,0:T(2,128)S(1)}, s32[2,8]{1,0:T(2,128)}, u32[]{:S(2)}) copy-start(s32[2,8]{1,0:T(2,128)} %param.14) | copy-start | bytes 196
  5.1 6.6 %copy-start.6 = (s32[9,32]{1,0:T(8,128)S(1)}, s32[9,32]{1,0:T(8,128)}, u32[]{:S(2)}) copy-start(s32[9,32]{1,0:T(8,128)} %param.13) | copy-start | bytes 3460
  5.1 6.7 %copy-start.8 = (u32[32]{0:T(128)S(1)}, u32[32]{0:T(128)}, u32[]{:S(2)}) copy-start(u32[32]{0:T(128)} %constant.119) | copy-start | bytes 388
  5.1 44.4 %copy-start = (bf16[256,256]{1,0:T(8,128)(2,1)S(1)}, bf16[256,256]{1,0:T(8,128)(2,1)}, u32[]{:S(2)}) copy-start(bf16[256,256]{1,0:T(8,128)(2,1)} %constant.108.clone.inv_high) | copy-start | bytes 393220
  5.1 44.4 %copy-start.1 = (bf16[256,256]{1,0:T(8,128)(2,1)S(1)}, bf16[256,256]{1,0:T(8,128)(2,1)}, u32[]{:S(2)}) copy-start(bf16[256,256]{1,0:T(8,128)(2,1)} %constant.109.clone.inv_low) | copy-start | bytes 393220
  5.1 44.3 %copy-start.2 = (bf16[256,256]{1,0:T(8,128)(2,1)S(1)}, bf16[256,256]{1,0:T(8,128)(2,1)}, u32[]{:S(2)}) copy-start(bf16[256,256]{1,0:T(8,128)(2,1)} %constant.110.clone.back_high) | copy-start | bytes 393220
  5.1 44.3 %copy-start.3 = (bf16[256,256]{1,0:T(8,128)(2,1)S(1)}, bf16[256,256]{1,0:T(8,128)(2,1)}, u32[]{:S(2)}) copy-start(bf16[256,256]{1,0:T(8,128)(2,1)} %constant.111.clone.back_low) | copy-start | bytes 393220
  5.1 44.3 %copy-start.4 = (f32[256,1]{1,0:T(8,128)S(1)}, f32[256,1]{1,0:T(8,128)}, u32[]{:S(2)}) copy-start(f32[256,1]{1,0:T(8,128)} %constant.112.clone.diag) | copy-start | bytes 3076
  5.1 44.3 %all-to-all-start = ((f32[8,192,256]{2,1,0:T(8,128)}), f32[8,192,256]{2,1,0:T(8,128)S(1)}, u32[]{:S(2)}, u32[]{:S(2)}) async-start(f32[8,192,256]{2,1,0:T(8,128)} %bitcast.23), calls=%async_computation | async-start | bytes 3145728 | tf_op jit(solution)/shard_map/all_to_all | solution.py:176
  51.8 4.9 %copy-start.5 = (f32[9,64,64]{2,1,0:T(8,128)S(1)}, f32[9,64,64]{2,1,0:T(8,128)}, u32[]{:S(2)}) copy-start(f32[9,64,64]{2,1,0:T(8,128)} %param.12) | copy-start | bytes 442372
  51.8 24.9 %all-to-all-start.1 = ((f32[32,24,256]{2,1,0:T(8,128)}), f32[32,24,256]{2,1,0:T(8,128)S(1)}, u32[]{:S(2)}, u32[]{:S(2)}) async-start(f32[32,24,256]{2,1,0:T(8,128)} %shard_map.100), calls=%async_computation.1 | async-start | bytes 1572864 | tf_op jit(solution)/shard_map/all_to_all | solution.py:189

commit v2 on v1

--- a/solution.py
+++ b/solution.py
@@ -9,6 +9,7 @@
 from jax.sharding import PartitionSpec as P
 
 CHEB = 4
+PARTS = ((0, 2), (2, 3))
 F32 = jnp.float32
 BF16 = jnp.bfloat16
 
@@ -41,7 +42,7 @@
     return tables
 
 
-def lines_kernel(chunk, lines, inv_high, inv_low, back_high, back_low, diag, out):
+def lines_kernel(chunk, lines, inv_high, inv_low, back_high, back_low, diag, *outs):
     count = diag.shape[0]
     columns = lines.shape[-1]
     planes = []
@@ -54,10 +55,13 @@
         cross = planes[one] * planes[3 + two] - planes[two] * planes[3 + one]
         forcing = dot3(back_high[...], back_low[...], cross)
         rhs = (lines[:, 0, part].reshape(count, columns) + forcing) * diag[...]
-        if chunk % 8 == 0:
-            out[:, part * chunk : (part + 1) * chunk, :] = rhs.reshape(count // chunk, chunk, columns)
-        else:
-            out[part] = rhs
+        for out, (begin, end) in zip(outs, PARTS):
+            if begin <= part < end:
+                at = part - begin
+                if chunk % 8 == 0:
+                    out[:, at * chunk : (at + 1) * chunk, :] = rhs.reshape(count // chunk, chunk, columns)
+                else:
+                    out[at] = rhs
 
 
 def cheb_kernel(group, sides, refs, rhs, weights, scale, out, fields, resid, solution, rows_in, wide):
@@ -134,8 +138,7 @@
     elem_local = merged // points
     per_source = columns // points
     chunk = count // devices
-    rows = 3 * chunk
-    rows_up = -(-rows // 8) * 8
+    aligned = chunk % 8 == 0
 
     tables = jnp.concatenate([nbr_ref.reshape(-1), send_list.reshape(-1)])
     tables = lax.all_gather(tables, "dom")
@@ -176,47 +179,61 @@
     both = lax.all_to_all(both, "mode", split_axis=0, concat_axis=0, tiled=True)
     lines = both.reshape(mode_size, 2, 3, 2 * modes_dev, columns)
 
-    aligned = chunk % 8 == 0
-    rhs = pl.pallas_call(
+    made = pl.pallas_call(
         functools.partial(lines_kernel, chunk),
-        out_shape=jax.ShapeDtypeStruct(
-            (devices, rows, columns) if aligned else (3, count, columns), F32
-        ),
-        compiler_params=pltpu.CompilerParams(vmem_limit_bytes=40 * 2**20),
+        out_shape=[
+            jax.ShapeDtypeStruct(
+                (devices, (end - begin) * chunk, columns) if aligned else (end - begin, count, columns), F32
+            )
+            for begin, end in PARTS
+        ],
+        compiler_params=pltpu.CompilerParams(vmem_limit_bytes=24 * 2**20),
+        cost_estimate=pl.CostEstimate(flops=2 * 27 * count * count * columns, bytes_accessed=2**21, transcendentals=0),
     )(lines, *(jnp.asarray(t) for t in spanwise_tables(modes_all)), jnp.asarray(inv_diag[:, None]))
-    if not aligned:
-        rhs = jnp.swapaxes(rhs.reshape(3, devices, chunk, columns), 0, 1).reshape(devices, rows, columns)
-    rhs = lax.all_to_all(rhs, ("mode", "dom"), split_axis=0, concat_axis=0, tiled=True)
-    if rows_up != rows:
-        rhs = jnp.pad(rhs, ((0, 0), (0, rows_up - rows), (0, 0)))
 
     me = lax.axis_index("mode") * dom_size + lax.axis_index("dom")
     mode_ids = (me * chunk + jnp.arange(chunk, dtype=jnp.int32)) // 2
     wave = mode_ids.astype(F32) / modes_all
-    scale = jnp.tile(1.0 / (1.0 + 4.0 * wave * wave), 3)
-    scale = jnp.pad(scale, (0, rows_up - rows))
-    scale = jnp.broadcast_to(scale[:, None], (rows_up, 128))
-
-    group = min(32, devices)
-    held = (devices * per_source, rows_up, 128)
+    own_diag = 1.0 / (1.0 + 4.0 * wave * wave)
     vmem = pl.BlockSpec(memory_space=pltpu.VMEM)
-    out = pl.pallas_call(
-        functools.partial(cheb_kernel, group, dom_size),
-        out_shape=jax.ShapeDtypeStruct((dom_size, rows_up, merged), F32),
-        in_specs=[pl.BlockSpec(memory_space=pltpu.SMEM)] + [vmem] * 3,
-        out_specs=vmem,
-        scratch_shapes=[
-            pltpu.VMEM((2, *held), F32),
-            pltpu.VMEM(held, F32),
-            pltpu.VMEM(held, F32),
-            pltpu.VMEM((group * rows_up, slots * points), F32),
-            pltpu.VMEM((slots * points, 256), BF16),
-        ],
-        compiler_params=pltpu.CompilerParams(vmem_limit_bytes=48 * 2**20),
-    )(chosen, rhs, weights, scale)
-    out = lax.all_to_all(out[:, :rows], "dom", split_axis=0, concat_axis=0, tiled=True)
-    out = jnp.swapaxes(out.reshape(dom_size, 3, chunk, merged), 0, 1)
-    return out.reshape(3, modes_dev, 2, merged)
+    pieces = []
+    made = list(made)
+    for part, (begin, end) in enumerate(PARTS):
+        rhs = made[part]
+        rows = (end - begin) * chunk
+        rows_up = -(-rows // 8) * 8
+        if not aligned:
+            rhs = jnp.swapaxes(rhs.reshape(end - begin, devices, chunk, columns), 0, 1)
+            rhs = rhs.reshape(devices, rows, columns)
+        rhs = lax.all_to_all(rhs, ("mode", "dom"), split_axis=0, concat_axis=0, tiled=True)
+        if part + 1 < len(PARTS):
+            rhs, made[part + 1] = lax.optimization_barrier((rhs, made[part + 1]))
+        if rows_up != rows:
+            rhs = jnp.pad(rhs, ((0, 0), (0, rows_up - rows), (0, 0)))
+        scale = jnp.pad(jnp.tile(own_diag, end - begin), (0, rows_up - rows))
+        scale = jnp.broadcast_to(scale[:, None], (rows_up, 128))
+        group = min(32, devices)
+        held = (devices * per_source, rows_up, 128)
+        out = pl.pallas_call(
+            functools.partial(cheb_kernel, group, dom_size),
+            out_shape=jax.ShapeDtypeStruct((dom_size, rows_up, merged), F32),
+            in_specs=[pl.BlockSpec(memory_space=pltpu.SMEM)] + [vmem] * 3,
+            out_specs=vmem,
+            scratch_shapes=[
+                pltpu.VMEM((2, *held), F32),
+                pltpu.VMEM(held, F32),
+                pltpu.VMEM(held, F32),
+                pltpu.VMEM((group * rows_up, slots * points), F32),
+                pltpu.VMEM((slots * points, 256), BF16),
+            ],
+            compiler_params=pltpu.CompilerParams(vmem_limit_bytes=32 * 2**20),
+            cost_estimate=pl.CostEstimate(
+                flops=rows_up * 4 * 10**8, bytes_accessed=2**20, transcendentals=0
+            ),
+        )(chosen, rhs, weights, scale)
+        out = lax.all_to_all(out[:, :rows], "dom", split_axis=0, concat_axis=0, tiled=True)
+        pieces.append(jnp.swapaxes(out.reshape(dom_size, end - begin, chunk, merged), 0, 1))
+    return jnp.concatenate(pieces, axis=0).reshape(3, modes_dev, 2, merged)
 
 
 def solution(mesh):

time: 106 us -> 114 us (1.075)
  blocking collectives: 21.4 us -> 7.48 us
  starting transfers between devices: 9.98 us -> 20.6 us
  Pallas kernels: 16.3 us -> 26.2 us
  other arithmetic: 3.53 us -> 4.82 us
    all_to_all x1 -> x0, blocking collectives: 13.9 us -> none  [shards(): lax.all_to_all(out[:, :rows], 'dom', split_axis=0, concat_axis=0, tiled=T...]
    pallas_call x1 -> x2, Pallas kernels: 14 us -> 24 us  [shards(): pl.pallas_call(functools.partial(cheb_kernel, group, dom_size), out_shape...]
    all_to_all x0 -> x2, starting transfers between devices: none -> 8.03 us  [shards(): lax.all_to_all(out[:, :rows], 'dom', split_axis=0, concat_axis=0, tiled=T...]
    all_to_all x0 -> x2, waiting for transfers between devices: none -> 5.02 us  [shards(): lax.all_to_all(out[:, :rows], 'dom', split_axis=0, concat_axis=0, tiled=T...]
    all_to_all x1 -> x2, waiting for transfers between devices: 19.5 us -> 14.5 us  [shards(): lax.all_to_all(rhs, ('mode', 'dom'), split_axis=0, concat_axis=0, tiled=T...]
    all_to_all x1 -> x2, starting transfers between devices: 3.51 us -> 6.09 us  [shards(): lax.all_to_all(rhs, ('mode', 'dom'), split_axis=0, concat_axis=0, tiled=T...]
    reshape x1 -> x0, local copies, waits for them, and re-layouts: 1.34 us -> none  [shards(): return out.reshape(3, modes_dev, 2, merged)]
    concatenate x0 -> x1, other arithmetic: none -> 1.29 us  [shards(): return jnp.concatenate(pieces, axis=0).reshape(3, modes_dev, 2, merged)]
  transfers between devices with their start and end apart: 2 -> 5, of which waited for: 2 -> 3; matrix products, arithmetic and copies ran while one was open for 3% -> 3% of each run, Pallas kernels for 0% -> 21%
where the time goes in v2:
time: 114 us; the launch traced here: 113 us
  waiting for transfers between devices  47.9 us (42%)
  Pallas kernels  26.2 us (23%)
  starting transfers between devices  20.6 us (18%)
  blocking collectives  7.48 us (7%)
  local copies, waits for them, and re-layouts  5.16 us (5%)
  other arithmetic  4.82 us (4%)
    all_to_all x1, waiting for transfers between devices, shards(): both = lax.all_to_all(both, 'mode', split_axis=0, concat_axis=0, tiled=True)  28.4 us
    pallas_call x2, Pallas kernels, shards(): pl.pallas_call(functools.partial(cheb_kernel, group, dom_size), out_shape...  24 us
    all_to_all x2, waiting for transfers between devices, shards(): lax.all_to_all(rhs, ('mode', 'dom'), split_axis=0, concat_axis=0, tiled=T...  14.5 us
    all_to_all x2, starting transfers between devices, shards(): lax.all_to_all(out[:, :rows], 'dom', split_axis=0, concat_axis=0, tiled=T...  8.03 us
    unnamed x1, blocking collectives  7.48 us
    all_to_all x1, starting transfers between devices, shards(): both = lax.all_to_all(both, 'mode', split_axis=0, concat_axis=0, tiled=True)  6.47 us
    all_to_all x2, starting transfers between devices, shards(): lax.all_to_all(rhs, ('mode', 'dom'), split_axis=0, concat_axis=0, tiled=T...  6.09 us
    all_to_all x2, waiting for transfers between devices, shards(): lax.all_to_all(out[:, :rows], 'dom', split_axis=0, concat_axis=0, tiled=T...  5.02 us
  transfers between devices with their start and end apart: 5, of which 3 were waited for; matrix products, arithmetic and copies ran while one was open for 3% of the time, Pallas kernels for 21%

profile of v2, /device:TPU:0, one launch (start us, length us, event | category | flops | bytes accessed | tf_op | source)
XLA Modules:
  0.0 113.1 jit_solution(18055151472282716354)
XLA Ops:
  0.0 2.2 %pad_maximum_fusion = f32[2,3,16,2,2048]{4,3,2,1,0:T(2,128)S(1)} fusion(f32[1,3,16,2,2048]{4,3,2,1,0:T(2,128)} %bitcast.26, f32[1,3,16,2,2048]{4,3,2,1,0:T(2,128)} %bitcast.27), kind=kLoop, calls=%fused_computation | loop fusion | flops 393216 | bytes 3145728 | tf_op jit(solution)/shard_map/stack | solution.py:177
  2.2 1.3 %reshape.90 = f32[192,8,256]{2,1,0:T(8,128)S(1)} reshape(f32[2,3,16,2,2048]{4,3,2,1,0:T(2,128)S(1)} %pad_maximum_fusion) | data formatting | bytes 3145728 | tf_op jit(solution)/shard_map/reshape | solution.py:177
  3.4 1.7 %copy.29 = f32[192,8,256]{2,0,1:T(8,128)} copy(f32[192,8,256]{2,1,0:T(8,128)S(1)} %reshape.90) | data formatting | bytes 3145728 | tf_op jit(solution)/shard_map/reshape | solution.py:177
  5.1 0.0 copy-start.1
  5.1 0.0 copy-start.2
  5.1 0.0 copy-start.3
  5.2 0.0 copy-start.4
  5.2 6.5 %all-to-all-start = ((f32[8,192,256]{2,1,0:T(8,128)}), f32[8,192,256]{2,1,0:T(8,128)S(1)}, u32[]{:S(2)}, u32[]{:S(2)}) async-start(f32[8,192,256]{2,1,0:T(8,128)} %bitcast.23), calls=%async_computation | async-start | bytes 3145728 | tf_op jit(solution)/shard_map/all_to_all | solution.py:179
  11.6 0.0 copy-done.7
  11.6 0.1 reshape.86
  11.7 0.0 copy-done.6
  11.7 0.1 reshape.85
  11.8 0.0 copy-done.8
  11.8 0.6 dynamic-slice
  13.0 0.2 add_dynamic-update-slice_fusion
  13.2 7.5 %all-reduce.2 = s32[1216]{0:T(1024)S(1)} all-reduce(s32[1216]{0:T(1024)S(1)} %add_dynamic-update-slice_fusion), channel_id=2, replica_groups=mesh['mode'=8,'dom'=4] {'dom'}, use_global_device_ids=true, to_apply=%add.2 | all-reduce | flops 1216 | bytes 9728
  20.7 0.1 reshape.94
  20.8 0.1 slice.37
  20.9 0.1 reshape.87
  21.0 0.1 eq.20
  21.1 28.4 %all-to-all-done = f32[8,192,256]{2,1,0:T(8,128)S(1)} async-done(((f32[8,192,256]{2,1,0:T(8,128)}), f32[8,192,256]{2,1,0:T(8,128)S(1)}, u32[]{:S(2)}, u32[]{:S(2)}) %all-to-all-start) | async-done | bytes 1572896 | tf_op jit(solution)/shard_map/all_to_all | solution.py:179
  49.5 0.0 copy-done
  49.5 0.0 copy-done.1
  49.5 0.0 copy-done.2
  49.5 2.2 %shard_map.100 = (f32[32,16,256]{2,1,0:T(8,128)}, f32[32,8,256]{2,1,0:T(8,128)}) custom-call(f32[8,2,3,32,256]{4,3,2,1,0:T(8,128)S(1)} %bitcast.22, bf16[256,256]{1,0:T(8,128)(2,1)S(1)} %copy-done, bf16[256,256]{1,0:T(8,128)(2,1)S(1)} %copy-done.1, bf16[256,256]{1,0:T(8,128)(2,1)S(1)} %copy-done.2, bf16[256,256]{1,0:T(8,128)(2,1)S(1)} %copy-done.3, ...), custom_call_target="tpu_custom_call" | custom-call | flops 905969664 | bytes 2097152 | tf_op jit(solution)/shard_map/pallas_call | solution.py:182
  51.7 3.5 %all-to-all-start.1 = ((f32[32,16,256]{2,1,0:T(8,128)}), f32[32,16,256]{2,1,0:T(8,128)S(1)}, u32[]{:S(2)}, u32[]{:S(2)}) async-start(f32[32,16,256]{2,1,0:T(8,128)} %get-tuple-element.9), calls=%async_computation.1 | async-start | bytes 1048576 | tf_op jit(solution)/shard_map/all_to_all | solution.py:208
  55.2 0.1 add_add_fusion
  55.3 0.9 select_reduce_fusion
  56.2 0.1 copy.27
  56.4 0.1 copy.24.refs
  56.4 0.0 copy-done.5
  56.4 0.2 copy.23
  56.6 0.1 broadcast_in_dim.53
  56.7 0.2 pad_maximum_fusion.2.weights
  56.9 14.5 %all-to-all-done.1.rhs = f32[32,16,256]{2,1,0:T(8,128)S(1)} async-done(((f32[32,16,256]{2,1,0:T(8,128)}), f32[32,16,256]{2,1,0:T(8,128)S(1)}, u32[]{:S(2)}, u32[]{:S(2)}) %all-to-all-start.1) | async-done | bytes 524320 | tf_op jit(solution)/shard_map/all_to_all | solution.py:208
  71.4 2.6 %all-to-all-start.3 = ((f32[32,8,256]{2,1,0:T(8,128)}), f32[32,8,256]{2,1,0:T(8,128)S(1)}, u32[]{:S(2)}, u32[]{:S(2)}) async-start(f32[32,8,256]{2,1,0:T(8,128)} %get-tuple-element.12), calls=%async_computation.3 | async-start | bytes 524288 | tf_op jit(solution)/shard_map/all_to_all | solution.py:208
  74.0 0.1 broadcast_in_dim.54.scale
  74.1 12.4 %shard_map.101 = f32[4,16,2048]{2,1,0:T(8,128)} custom-call(s32[10,128]{1,0:T(8,128)S(1)} %copy.24.refs, f32[32,16,256]{2,1,0:T(8,128)S(1)} %all-to-all-done.1.rhs, f32[640,128]{1,0:T(8,128)S(1)} %pad_maximum_fusion.2.weights, f32[16,128]{1,0:T(8,128)S(1)} %broadcast_in_dim.54.scale), custom_call_target="tpu_custom_call" | custom-call | flops 6400000000 | bytes 1048576 | tf_op jit(solution)/shard_map/pallas_call | solution.py:217
  86.5 0.0 all-to-all-done.3.rhs
  86.5 3.8 %all-to-all-start.2 = ((f32[4,16,2048]{2,1,0:T(8,128)}), f32[4,16,2048]{2,1,0:T(8,128)S(1)}, u32[]{:S(2)}, u32[]{:S(2)}) async-start(f32[4,16,2048]{2,1,0:T(8,128)} %shard_map.101), calls=%async_computation.2 | async-start | bytes 1048576 | tf_op jit(solution)/shard_map/all_to_all | solution.py:234
  90.4 0.1 broadcast_in_dim.55.scale
  90.4 11.6 %shard_map.102 = f32[4,8,2048]{2,1,0:T(8,128)} custom-call(s32[10,128]{1,0:T(8,128)S(1)} %copy.24.refs, f32[32,8,256]{2,1,0:T(8,128)S(1)} %all-to-all-done.3.rhs, f32[640,128]{1,0:T(8,128)S(1)} %pad_maximum_fusion.2.weights, f32[8,128]{1,0:T(8,128)S(1)} %broadcast_in_dim.55.scale), custom_call_target="tpu_custom_call" | custom-call | flops 3200000000 | bytes 1048576 | tf_op jit(solution)/shard_map/pallas_call | solution.py:217
  102.1 0.0 all-to-all-done.2
  102.1 4.2 %all-to-all-start.4 = ((f32[4,8,2048]{2,1,0:T(8,128)}), f32[4,8,2048]{2,1,0:T(8,128)S(1)}, u32[]{:S(2)}, u32[]{:S(2)}) async-start(f32[4,8,2048]{2,1,0:T(8,128)} %shard_map.102), calls=%async_computation.4 | async-start | bytes 524288 | tf_op jit(solution)/shard_map/all_to_all | solution.py:234
  106.3 0.3 concatenate.30
  106.6 5.0 %all-to-all-done.4 = f32[4,8,2048]{2,1,0:T(8,128)S(1)} async-done(((f32[4,8,2048]{2,1,0:T(8,128)}), f32[4,8,2048]{2,1,0:T(8,128)S(1)}, u32[]{:S(2)}, u32[]{:S(2)}) %all-to-all-start.4) | async-done | bytes 262176 | tf_op jit(solution)/shard_map/all_to_all | solution.py:234
  111.6 0.1 concatenate.31
  111.8 1.3 %pad_maximum_fusion.1 = f32[3,16,2,2048]{3,2,1,0:T(2,128)} fusion(f32[1,16,2,2048]{3,2,1,0:T(2,128)S(1)} %concatenate.31, f32[2,16,2,2048]{3,2,1,0:T(2,128)S(1)} %concatenate.30), kind=kLoop, calls=%fused_computation.2 | loop fusion | flops 196608 | bytes 1572864 | tf_op jit(solution)/shard_map/concatenate | solution.py:236
  (24 shorter events, 0.2 us)
Async XLA Ops:
  5.1 6.5 %copy-start.7 = (s32[2,8]{1,0:T(2,128)S(1)}, s32[2,8]{1,0:T(2,128)}, u32[]{:S(2)}) copy-start(s32[2,8]{1,0:T(2,128)} %param.14) | copy-start | bytes 196
  5.1 6.6 %copy-start.6 = (s32[9,32]{1,0:T(8,128)S(1)}, s32[9,32]{1,0:T(8,128)}, u32[]{:S(2)}) copy-start(s32[9,32]{1,0:T(8,128)} %param.13) | copy-start | bytes 3460
  5.1 6.7 %copy-start.8 = (u32[32]{0:T(128)S(1)}, u32[32]{0:T(128)}, u32[]{:S(2)}) copy-start(u32[32]{0:T(128)} %constant.119) | copy-start | bytes 388
  5.1 44.4 %copy-start = (bf16[256,256]{1,0:T(8,128)(2,1)S(1)}, bf16[256,256]{1,0:T(8,128)(2,1)}, u32[]{:S(2)}) copy-start(bf16[256,256]{1,0:T(8,128)(2,1)} %constant.108.clone.inv_high) | copy-start | bytes 393220
  5.1 44.4 %copy-start.1 = (bf16[256,256]{1,0:T(8,128)(2,1)S(1)}, bf16[256,256]{1,0:T(8,128)(2,1)}, u32[]{:S(2)}) copy-start(bf16[256,256]{1,0:T(8,128)(2,1)} %constant.109.clone.inv_low) | copy-start | bytes 393220
  5.1 44.3 %copy-start.2 = (bf16[256,256]{1,0:T(8,128)(2,1)S(1)}, bf16[256,256]{1,0:T(8,128)(2,1)}, u32[]{:S(2)}) copy-start(bf16[256,256]{1,0:T(8,128)(2,1)} %constant.110.clone.back_high) | copy-start | bytes 393220
  5.1 44.3 %copy-start.3 = (bf16[256,256]{1,0:T(8,128)(2,1)S(1)}, bf16[256,256]{1,0:T(8,128)(2,1)}, u32[]{:S(2)}) copy-start(bf16[256,256]{1,0:T(8,128)(2,1)} %constant.111.clone.back_low) | copy-start | bytes 393220
  5.2 44.3 %copy-start.4 = (f32[256,1]{1,0:T(8,128)S(1)}, f32[256,1]{1,0:T(8,128)}, u32[]{:S(2)}) copy-start(f32[256,1]{1,0:T(8,128)} %constant.112.clone.diag) | copy-start | bytes 3076
  5.2 44.3 %all-to-all-start = ((f32[8,192,256]{2,1,0:T(8,128)}), f32[8,192,256]{2,1,0:T(8,128)S(1)}, u32[]{:S(2)}, u32[]{:S(2)}) async-start(f32[8,192,256]{2,1,0:T(8,128)} %bitcast.23), calls=%async_computation | async-start | bytes 3145728 | tf_op jit(solution)/shard_map/all_to_all | solution.py:179
  51.7 4.8 %copy-start.5 = (f32[9,64,64]{2,1,0:T(8,128)S(1)}, f32[9,64,64]{2,1,0:T(8,128)}, u32[]{:S(2)}) copy-start(f32[9,64,64]{2,1,0:T(8,128)} %param.12) | copy-start | bytes 442372
  51.7 19.8 %all-to-all-start.1 = ((f32[32,16,256]{2,1,0:T(8,128)}), f32[32,16,256]{2,1,0:T(8,128)S(1)}, u32[]{:S(2)}, u32[]{:S(2)}) async-start(f32[32,16,256]{2,1,0:T(8,128)} %get-tuple-element.9), calls=%async_computation.1 | async-start | bytes 1048576 | tf_op jit(solution)/shard_map/all_to_all | solution.py:208
  71.4 15.1 %all-to-all-start.3 = ((f32[32,8,256]{2,1,0:T(8,128)}), f32[32,8,256]{2,1,0:T(8,128)S(1)}, u32[]{:S(2)}, u32[]{:S(2)}) async-start(f32[32,8,256]{2,1,0:T(8,128)} %get-tuple-element.12), calls=%async_computation.3 | async-start | bytes 524288 | tf_op jit(solution)/shard_map/all_to_all | solution.py:208
  86.5 15.5 %all-to-all-start.2 = ((f32[4,16,2048]{2,1,0:T(8,128)}), f32[4,16,2048]{2,1,0:T(8,128)S(1)}, u32[]{:S(2)}, u32[]{:S(2)}) async-start(f32[4,16,2048]{2,1,0:T(8,128)} %shard_map.101), calls=%async_computation.2 | async-start | bytes 1048576 | tf_op jit(solution)/shard_map/all_to_all | solution.py:234
  102.1 9.6 %all-to-all-start.4 = ((f32[4,8,2048]{2,1,0:T(8,128)}), f32[4,8,2048]{2,1,0:T(8,128)S(1)}, u32[]{:S(2)}, u32[]{:S(2)}) async-start(f32[4,8,2048]{2,1,0:T(8,128)} %shard_map.102), calls=%async_computation.4 | async-start | bytes 524288 | tf_op jit(solution)/shard_map/all_to_all | solution.py:234

commit v3 on v1

--- a/solution.py
+++ b/solution.py
@@ -65,6 +65,7 @@
     per_source = columns // 64
     elems = sources * per_source
     slots = rows_in.shape[1] // 64
+    used = refs.shape[0] // elems
     lane = lax.broadcasted_iota(jnp.int32, (1, 1, 128), 2)
     lower = lane < 64
     first, second = fields.at[0], fields.at[1]
@@ -84,16 +85,14 @@
 
         def body(index, carry, step=step, now=now, later=later, rho=rho, rho_next=rho_next, last=last):
             low_lane = lower[0]
+            base = index * (group * used)
             for j in range(group):
-                elem = index * group + j
                 for pair in range(slots // 2):
-                    a = refs[2 * pair, elem]
-                    b = refs[2 * pair + 1, elem]
-                    left = now[a]
-                    right = now[b]
-                    rows_in[j * rows : (j + 1) * rows, pair * 128 : (pair + 1) * 128] = jnp.where(
-                        low_lane, left, right
-                    )
+                    at = base + (j * used + 2 * pair)
+                    value = now[refs[at]]
+                    if 2 * pair + 1 < used:
+                        value = jnp.where(low_lane, value, now[refs[at + 1]])
+                    rows_in[j * rows : (j + 1) * rows, pair * 128 : (pair + 1) * 128] = value
             high, low = split(rows_in[...])
             total = dot(high, wide[...])
             total = total[:, :128] + total[:, 128:] + dot(low, wide[:, :128])
@@ -159,10 +158,9 @@
     chosen = jnp.sum(
         jnp.where(refs[..., None] == entries, extended[:, None, None, :], 0), axis=-1
     )
-    chosen = jnp.pad(chosen, ((0, 0), (0, slot_count % 2), (0, 0)))
-    slots = chosen.shape[1]
-    chosen = chosen.reshape(dom_size, slots, mode_size, per_source).transpose(1, 3, 2, 0)
-    chosen = chosen.reshape(slots, devices * per_source)
+    slots = slot_count + slot_count % 2
+    chosen = chosen.reshape(dom_size, slot_count, mode_size, per_source).transpose(3, 2, 0, 1)
+    chosen = chosen.reshape(-1)
 
     weights = jnp.swapaxes(blocks, 1, 2).reshape(slot_count * points, points)
     weights = jnp.pad(weights, ((0, (slots - slot_count) * points), (0, 0)))
@@ -197,7 +195,7 @@
     scale = jnp.pad(scale, (0, rows_up - rows))
     scale = jnp.broadcast_to(scale[:, None], (rows_up, 128))
 
-    group = min(32, devices)
+    group = min(64, 2 * devices)
     held = (devices * per_source, rows_up, 128)
     vmem = pl.BlockSpec(memory_space=pltpu.VMEM)
     out = pl.pallas_call(

time: 106 us -> 109 us (1.028)
  other arithmetic: 3.53 us -> 5.2 us
  local copies, waits for them, and re-layouts: 5.98 us -> 7.36 us
    another operation x1, other arithmetic: 2.18 us -> 3.85 us  [shards(): jnp.stack([velocity, vorticity])]
    reshape x2, local copies, waits for them, and re-layouts: 2.89 us -> 4.17 us  [shards(): jnp.stack([velocity, vorticity])]
where the time goes in v3:
time: 109 us
  waiting for transfers between devices  47.7 us (44%)
  blocking collectives  21.3 us (20%)
  Pallas kernels  15.9 us (15%)
  starting transfers between devices  10.2 us (9%)
  local copies, waits for them, and re-layouts  7.36 us (7%)
  other arithmetic  5.2 us (5%)
    all_to_all x1, waiting for transfers between devices, shards(): both = lax.all_to_all(both, 'mode', split_axis=0, concat_axis=0, tiled=True)  28.5 us
    all_to_all x1, waiting for transfers between devices, shards(): lax.all_to_all(rhs, ('mode', 'dom'), split_axis=0, concat_axis=0, tiled=T...  19.2 us
    all_to_all x1, blocking collectives, shards(): lax.all_to_all(out[:, :rows], 'dom', split_axis=0, concat_axis=0, tiled=T...  13.9 us
    pallas_call x1, Pallas kernels, shards(): pl.pallas_call(functools.partial(cheb_kernel, group, dom_size), out_shape...  13.6 us
    unnamed x1, blocking collectives  7.48 us
    all_to_all x1, starting transfers between devices, shards(): both = lax.all_to_all(both, 'mode', split_axis=0, concat_axis=0, tiled=True)  6.47 us
    reshape x2, local copies, waits for them, and re-layouts, shards(): jnp.stack([velocity, vorticity])  4.17 us
    another operation x1, other arithmetic, shards(): jnp.stack([velocity, vorticity])  3.85 us
  transfers between devices with their start and end apart: 2, of which 2 were waited for; matrix products, arithmetic and copies ran while one was open for 3% of the time, Pallas kernels for 0%

profile of v3, /device:TPU:0, one launch (start us, length us, event | category | flops | bytes accessed | tf_op | source)
XLA Modules:
  0.0 108.6 jit_solution(2661919973282038897)
XLA Ops:
  0.0 3.8 %pad_maximum_fusion = f32[2,3,16,2,2048]{4,3,2,1,0:T(2,128)} fusion(f32[1,3,16,2,2048]{4,3,2,1,0:T(2,128)} %bitcast.25, f32[1,3,16,2,2048]{4,3,2,1,0:T(2,128)} %bitcast.26), kind=kLoop, calls=%fused_computation | loop fusion | flops 393216 | bytes 3145728 | tf_op jit(solution)/shard_map/stack | solution.py:172
  3.8 2.5 %reshape.64 = f32[192,8,256]{2,1,0:T(8,128)S(1)} reshape(f32[2,3,16,2,2048]{4,3,2,1,0:T(2,128)} %pad_maximum_fusion) | data formatting | bytes 3145728 | tf_op jit(solution)/shard_map/reshape | solution.py:172
  6.4 1.6 %copy.24 = f32[192,8,256]{2,0,1:T(8,128)} copy(f32[192,8,256]{2,1,0:T(8,128)S(1)} %reshape.64) | data formatting | bytes 3145728 | tf_op jit(solution)/shard_map/reshape | solution.py:172
  8.0 0.0 copy-start.7
  8.0 0.0 copy-start.6
  8.0 0.0 copy-start.8
  8.0 0.0 copy-start
  8.0 0.0 copy-start.1
  8.0 0.0 copy-start.2
  8.1 0.0 copy-start.3
  8.1 0.0 copy-start.4
  8.1 6.5 %all-to-all-start = ((f32[8,192,256]{2,1,0:T(8,128)}), f32[8,192,256]{2,1,0:T(8,128)S(1)}, u32[]{:S(2)}, u32[]{:S(2)}) async-start(f32[8,192,256]{2,1,0:T(8,128)} %bitcast.22), calls=%async_computation | async-start | bytes 3145728 | tf_op jit(solution)/shard_map/all_to_all | solution.py:174
  14.6 0.0 copy-done.7
  14.6 0.1 reshape.60
  14.6 0.0 copy-done.6
  14.6 0.1 reshape.59
  14.7 0.0 copy-done.8
  14.7 0.6 dynamic-slice
  16.0 0.2 add_dynamic-update-slice_fusion
  16.2 7.5 %all-reduce.1 = s32[1216]{0:T(1024)S(1)} all-reduce(s32[1216]{0:T(1024)S(1)} %add_dynamic-update-slice_fusion), channel_id=2, replica_groups=mesh['mode'=8,'dom'=4] {'dom'}, use_global_device_ids=true, to_apply=%add.1 | all-reduce | flops 1216 | bytes 9728
  23.6 0.1 reshape.69
  23.7 0.1 slice.37
  23.8 0.1 reshape.61
  23.9 28.5 %all-to-all-done = f32[8,192,256]{2,1,0:T(8,128)S(1)} async-done(((f32[8,192,256]{2,1,0:T(8,128)}), f32[8,192,256]{2,1,0:T(8,128)S(1)}, u32[]{:S(2)}, u32[]{:S(2)}) %all-to-all-start) | async-done | bytes 1572896 | tf_op jit(solution)/shard_map/all_to_all | solution.py:174
  52.4 0.0 copy-done
  52.4 0.0 copy-done.1
  52.4 0.0 copy-done.2
  52.4 0.0 copy-done.3
  52.4 0.0 copy-done.4
  52.4 2.3 %shard_map.100 = f32[32,24,256]{2,1,0:T(8,128)} custom-call(f32[8,2,3,32,256]{4,3,2,1,0:T(8,128)S(1)} %bitcast.21, bf16[256,256]{1,0:T(8,128)(2,1)S(1)} %copy-done, bf16[256,256]{1,0:T(8,128)(2,1)S(1)} %copy-done.1, bf16[256,256]{1,0:T(8,128)(2,1)S(1)} %copy-done.2, bf16[256,256]{1,0:T(8,128)(2,1)S(1)} %copy-done.3, f32[256,1]{1,0:T(8,128)S(1)} %copy-done.4), custom_call_target="tpu_custom_call" | custom-call | tf_op jit(solution)/shard_map/pallas_call | solution.py:178
  54.8 0.0 copy-start.5
  54.8 3.7 %all-to-all-start.1 = ((f32[32,24,256]{2,1,0:T(8,128)}), f32[32,24,256]{2,1,0:T(8,128)S(1)}, u32[]{:S(2)}, u32[]{:S(2)}) async-start(f32[32,24,256]{2,1,0:T(8,128)} %shard_map.100), calls=%async_computation.1 | async-start | bytes 1572864 | tf_op jit(solution)/shard_map/all_to_all | solution.py:187
  58.5 0.1 eq.20
  58.7 0.1 add_add_fusion
  58.7 0.9 select_reduce_fusion
  59.6 0.1 copy.18
  59.8 0.2 reshape.63.refs
  60.0 0.0 copy-done.5
  60.0 0.1 copy.21
  60.2 0.1 broadcast_in_dim.47
  60.3 0.2 pad_maximum_fusion.1.weights
  60.4 19.2 %all-to-all-done.1.rhs = f32[32,24,256]{2,1,0:T(8,128)S(1)} async-done(((f32[32,24,256]{2,1,0:T(8,128)}), f32[32,24,256]{2,1,0:T(8,128)S(1)}, u32[]{:S(2)}, u32[]{:S(2)}) %all-to-all-start.1) | async-done | bytes 786464 | tf_op jit(solution)/shard_map/all_to_all | solution.py:187
  79.7 0.1 broadcast_in_dim.48.scale
  79.7 13.6 %shard_map.101 = f32[4,24,2048]{2,1,0:T(8,128)S(1)} custom-call(s32[1152]{0:T(1024)S(1)} %reshape.63.refs, f32[32,24,256]{2,1,0:T(8,128)S(1)} %all-to-all-done.1.rhs, f32[640,128]{1,0:T(8,128)S(1)} %pad_maximum_fusion.1.weights, f32[24,128]{1,0:T(8,128)S(1)} %broadcast_in_dim.48.scale), custom_call_target="tpu_custom_call" | custom-call | tf_op jit(solution)/shard_map/pallas_call | solution.py:201
  93.3 13.9 %all_to_all.15 = f32[4,24,2048]{2,1,0:T(8,128)S(1)} all-to-all(f32[4,24,2048]{2,1,0:T(8,128)S(1)} %shard_map.101), channel_id=1, replica_groups=mesh['mode'=8,'dom'=4] {'dom'}, dimensions={0} | all-to-all | bytes 1572864 | tf_op jit(solution)/shard_map/all_to_all | solution.py:215
  107.2 0.1 copy.22
  107.3 1.3 %reshape.68 = f32[3,16,2,2048]{3,2,1,0:T(2,128)} reshape(f32[3,4,8,2048]{3,2,1,0:T(8,128)S(1)} %copy.22) | data formatting | bytes 1572864 | tf_op jit(solution)/shard_map/reshape | solution.py:217
  (15 shorter events, 0.2 us)
Async XLA Ops:
  8.0 6.5 %copy-start.7 = (s32[2,8]{1,0:T(2,128)S(1)}, s32[2,8]{1,0:T(2,128)}, u32[]{:S(2)}) copy-start(s32[2,8]{1,0:T(2,128)} %param.14) | copy-start | bytes 196
  8.0 6.6 %copy-start.6 = (s32[9,32]{1,0:T(8,128)S(1)}, s32[9,32]{1,0:T(8,128)}, u32[]{:S(2)}) copy-start(s32[9,32]{1,0:T(8,128)} %param.13) | copy-start | bytes 3460
  8.0 6.7 %copy-start.8 = (u32[32]{0:T(128)S(1)}, u32[32]{0:T(128)}, u32[]{:S(2)}) copy-start(u32[32]{0:T(128)} %constant.117) | copy-start | bytes 388
  8.0 44.4 %copy-start = (bf16[256,256]{1,0:T(8,128)(2,1)S(1)}, bf16[256,256]{1,0:T(8,128)(2,1)}, u32[]{:S(2)}) copy-start(bf16[256,256]{1,0:T(8,128)(2,1)} %constant.108.clone.inv_high) | copy-start | bytes 393220
  8.0 44.4 %copy-start.1 = (bf16[256,256]{1,0:T(8,128)(2,1)S(1)}, bf16[256,256]{1,0:T(8,128)(2,1)}, u32[]{:S(2)}) copy-start(bf16[256,256]{1,0:T(8,128)(2,1)} %constant.109.clone.inv_low) | copy-start | bytes 393220
  8.0 44.3 %copy-start.2 = (bf16[256,256]{1,0:T(8,128)(2,1)S(1)}, bf16[256,256]{1,0:T(8,128)(2,1)}, u32[]{:S(2)}) copy-start(bf16[256,256]{1,0:T(8,128)(2,1)} %constant.110.clone.back_high) | copy-start | bytes 393220
  8.1 44.3 %copy-start.3 = (bf16[256,256]{1,0:T(8,128)(2,1)S(1)}, bf16[256,256]{1,0:T(8,128)(2,1)}, u32[]{:S(2)}) copy-start(bf16[256,256]{1,0:T(8,128)(2,1)} %constant.111.clone.back_low) | copy-start | bytes 393220
  8.1 44.3 %copy-start.4 = (f32[256,1]{1,0:T(8,128)S(1)}, f32[256,1]{1,0:T(8,128)}, u32[]{:S(2)}) copy-start(f32[256,1]{1,0:T(8,128)} %constant.112.clone.diag) | copy-start | bytes 3076
  8.1 44.3 %all-to-all-start = ((f32[8,192,256]{2,1,0:T(8,128)}), f32[8,192,256]{2,1,0:T(8,128)S(1)}, u32[]{:S(2)}, u32[]{:S(2)}) async-start(f32[8,192,256]{2,1,0:T(8,128)} %bitcast.22), calls=%async_computation | async-start | bytes 3145728 | tf_op jit(solution)/shard_map/all_to_all | solution.py:174
  54.8 5.2 %copy-start.5 = (f32[9,64,64]{2,1,0:T(8,128)S(1)}, f32[9,64,64]{2,1,0:T(8,128)}, u32[]{:S(2)}) copy-start(f32[9,64,64]{2,1,0:T(8,128)} %param.12) | copy-start | bytes 442372
  54.8 24.9 %all-to-all-start.1 = ((f32[32,24,256]{2,1,0:T(8,128)}), f32[32,24,256]{2,1,0:T(8,128)S(1)}, u32[]{:S(2)}, u32[]{:S(2)}) async-start(f32[32,24,256]{2,1,0:T(8,128)} %shard_map.100), calls=%async_computation.1 | async-start | bytes 1572864 | tf_op jit(solution)/shard_map/all_to_all | solution.py:187
